TPU v7x, 32 devices: a whole 2x2x4 slice. The times are simulated.
32 devices in a mesh: grp: 2 (over y), gx: 8 (over z, x), gy: 2 (over core).
Axes of the slice: x: 2, y: 2, z: 4, core: 2. Of those that a mesh axis runs over, the one named last changes fastest.
Arguments:
- activations: bfloat16 [256, 8192], P('grp', 'gx'), parts along dimension 0, may hold values from -6 to 6
- upstream: bfloat16 [256, 8192], P('grp', 'gx'), parts along dimension 0, may hold values from -6 to 6
- head_grad: bfloat16 [256, 8192], P('grp', 'gx'), parts along dimension 0, may hold values from -6 to 6
- target_mask: int32 [256], P('grp'), parts along dimension 0, may hold values 0 or 1
- gate_weight: bfloat16 [8192, 26624], P('gx', 'gy'), may hold values from -0.09375 to 0.09375
- up_weight: bfloat16 [8192, 26624], P('gx', 'gy'), may hold values from -0.09375 to 0.09375
- down_weight: bfloat16 [26624, 8192], P('gy', 'gx'), may hold values from -0.0546875 to 0.0546875
Outputs:
- input_grad: bfloat16 [256, 8192], P('grp', 'gx'), parts along dimension 0
There are 2 independent parts, one for each index of `grp`. A program takes and returns all parts, laid end to end along the dimension named above; an argument that names none is the same for every part. Nothing has to cross between parts.
All inputs are finite; a program needn't handle non-finite values.
Results may differ from a plain program's by a relative error of at most 0.0055.
Values may be sent and summed in bfloat16 or wider, within the bound.
A program may use at most 448 MiB of HBM per device.

v0:
```python
import jax
import jax.numpy as jnp
from jax import lax
from jax.sharding import PartitionSpec as P


def transposed(left, weight):
    return lax.dot_general(
        left, weight, (((1,), (1,)), ((), ())), preferred_element_type=jnp.float32
    )


def swiglu_grads(gate_proj, up_proj, hidden_grad):
    sigmoid_gate = jax.nn.sigmoid(gate_proj)
    gate_grad = hidden_grad * up_proj * sigmoid_gate * (1.0 + gate_proj * (1.0 - sigmoid_gate))
    up_grad = hidden_grad * gate_proj * sigmoid_gate
    return (gate_grad.astype(jnp.bfloat16), up_grad.astype(jnp.bfloat16))


def shards(activations, upstream, head_grad, target_mask, gate_weight, up_weight, down_weight):
    weights_mask = target_mask.astype(jnp.float32)[:, None]
    cotangent = (
        upstream.astype(jnp.float32) + weights_mask * head_grad.astype(jnp.float32)
    ).astype(jnp.bfloat16)
    gate_units, up_units = (
        lax.all_to_all(gate_weight, "gx", split_axis=1, concat_axis=0, tiled=True),
        lax.all_to_all(up_weight, "gx", split_axis=1, concat_axis=0, tiled=True),
    )
    down_units = lax.all_to_all(down_weight, "gx", split_axis=0, concat_axis=1, tiled=True)
    whole_rows, whole_cot = (
        lax.all_gather(activations, "gx", axis=1, tiled=True),
        lax.all_gather(cotangent, "gx", axis=1, tiled=True),
    )
    gate_proj = jnp.dot(whole_rows, gate_units, preferred_element_type=jnp.float32)
    up_proj = jnp.dot(whole_rows, up_units, preferred_element_type=jnp.float32)
    hidden_grad = transposed(whole_cot, down_units)
    gate_grad, up_grad = swiglu_grads(gate_proj, up_proj, hidden_grad)
    partial_grad = transposed(gate_grad, gate_units) + transposed(up_grad, up_units)
    feature_share = lax.psum_scatter(partial_grad, "gx", scatter_dimension=1, tiled=True)
    total_grad = lax.psum(feature_share, "gy")
    return total_grad.astype(jnp.bfloat16)


def solution(mesh):
    in_specs = (
        P("grp", "gx"),
        P("grp", "gx"),
        P("grp", "gx"),
        P("grp"),
        P("gx", "gy"),
        P("gx", "gy"),
        P("gy", "gx"),
    )
    out_specs = P("grp", "gx")
    return jax.shard_map(shards, mesh=mesh, in_specs=in_specs, out_specs=out_specs, check_vma=False)
```

profile of v0, /device:TPU:0, one launch (start us, length us, event | category | flops | bytes accessed | tf_op | source)
XLA Modules:
  0.0 2066.6 jit_solution(6756469074403025188)
XLA Ops:
  6.5 35.9 %copy.11 = bf16[1024,13312]{0,1:T(8,128)(2,1)} copy(bf16[1024,13312]{1,0:T(8,128)(2,1)} %param.11) | data formatting | bytes 54525952 | tf_op args[4]
  42.5 598.9 %all_to_all.57 = bf16[1024,8,1664]{0,2,1:T(8,128)(2,1)} all-to-all(bf16[1024,8,1664]{0,2,1:T(8,128)(2,1)} %bitcast.24), channel_id=1, replica_groups=mesh['grp'=2,'gx'=8,'gy'=2] {'gx'}, dimensions={1} | all-to-all | bytes 54525952 | tf_op jit(solution)/shard_map/all_to_all | solution.py:26
  641.4 6.7 all-to-all-start
  648.1 36.0 %copy.9 = bf16[1024,13312]{0,1:T(8,128)(2,1)} copy(bf16[1024,13312]{1,0:T(8,128)(2,1)} %param.12) | data formatting | bytes 54525952 | tf_op args[5]
  684.1 551.3 %all-to-all-done = bf16[8,1664,1024]{2,1,0:T(8,128)(2,1)} async-done(((bf16[8,1664,1024]{2,1,0:T(8,128)(2,1)}), bf16[8,1664,1024]{2,1,0:T(8,128)(2,1)}, u32[]{:S(2)}, u32[]{:S(2)}) %all-to-all-start) | async-done | bytes 27263008 | tf_op jit(solution)/shard_map/all_to_all | solution.py:29
  1235.4 0.0 copy-start.3
  1235.4 0.0 copy-start.1
  1235.4 0.0 copy-start.2
  1235.4 6.7 all-to-all-start.1
  1242.1 0.0 all-gather.3.cloned.1.call-start
  1242.1 0.0 copy-done.3
  1242.2 0.0 copy-done.1
  1242.2 0.0 copy-done.2
  1242.2 0.9 add_convert_fusion
  1243.0 0.0 all-gather.3.cloned.1.call-update
  1243.1 0.0 all-gather.5.cloned.1.call-start
  1243.1 0.7 all-gather.5.cloned.1.call-update
  1243.8 0.0 reduce-scatter.2.cloned.1.call-start
  1243.9 35.6 %copy.12 = bf16[8,1024,1664]{2,1,0:T(8,128)(2,1)} copy(bf16[8,1024,1664]{1,2,0:T(8,128)(2,1)} %bitcast.22) | data formatting | bytes 54525952 | tf_op jit(solution)/shard_map/all_to_all | solution.py:26
  1279.4 34.8 %copy.8 = bf16[1664,8,1024]{0,2,1:T(8,128)(2,1)} copy(bf16[1664,8,1024]{2,0,1:T(8,128)(2,1)} %bitcast.1) | data formatting | bytes 54525952 | tf_op jit(solution)/shard_map/all_to_all | solution.py:29
  1314.2 548.1 %all-to-all-done.1 = bf16[1024,8,1664]{0,2,1:T(8,128)(2,1)} async-done(((bf16[1024,8,1664]{0,2,1:T(8,128)(2,1)}), bf16[1024,8,1664]{0,2,1:T(8,128)(2,1)}, u32[]{:S(2)}, u32[]{:S(2)}) %all-to-all-start.1) | async-done | bytes 27263008 | tf_op jit(solution)/shard_map/all_to_all | solution.py:27
  1862.2 34.8 %copy.10 = bf16[8,1024,1664]{2,1,0:T(8,128)(2,1)} copy(bf16[8,1024,1664]{1,2,0:T(8,128)(2,1)} %bitcast.4) | data formatting | bytes 54525952 | tf_op jit(solution)/shard_map/all_to_all | solution.py:27
  1897.1 0.0 all-gather.3.cloned.1.call-done
  1897.1 13.4 fusion.11
  1910.4 0.0 all-gather.5.cloned.1.call-done
  1910.4 0.0 copy-start
  1910.5 14.4 fusion.12
  1924.9 0.0 copy-done
  1924.9 26.2 %fusion.3 = f32[128,8192]{1,0:T(8,128)} fusion(bf16[8192,1664]{1,0:T(8,128)(2,1)} %bitcast.20, f32[128,1664]{1,0:T(8,128)S(1)} %fusion.11, bf16[128,8192]{1,0:T(8,128)(2,1)S(1)} %copy-done, bf16[8192,1664]{1,0:T(8,128)(2,1)} %bitcast.17, f32[128,1664]{1,0:T(8,128)} %fusion.12), kind=kOutput, calls=%fused_computation.5 | convolution fusion | flops 6981451776 | bytes 62521344 | tf_op jit(solution)/shard_map/dot_general | solution.py:8
  1951.1 16.0 convolution_add_fusion
  1967.1 0.0 reduce-scatter.2.cloned.1.call-update
  1967.1 86.9 %reduce-scatter.2.cloned.1.call-done = f32[128,1024]{1,0:T(8,128)} async-done(((f32[128,8192]{1,0:T(8,128)}), f32[128,1024]{1,0:T(8,128)}) %reduce-scatter.2.cloned.1.call-update) | async-done | bytes 524304 | tf_op jit(solution)/shard_map/reduce_scatter | solution.py:39
  2054.0 6.1 all-reduce.1
  (1 shorter events, 0.0 us)
Async XLA Ops:
  641.4 594.0 %all-to-all-start = ((bf16[8,1664,1024]{2,1,0:T(8,128)(2,1)}), bf16[8,1664,1024]{2,1,0:T(8,128)(2,1)}, u32[]{:S(2)}, u32[]{:S(2)}) async-start(bf16[8,1664,1024]{2,1,0:T(8,128)(2,1)} %bitcast.25), calls=%async_computation | async-start | bytes 54525952 | tf_op jit(solution)/shard_map/all_to_all | solution.py:29
  1235.4 6.8 copy-start.3
  1235.4 6.8 copy-start.1
  1235.4 6.8 copy-start.2
  1235.4 626.8 %all-to-all-start.1 = ((bf16[1024,8,1664]{0,2,1:T(8,128)(2,1)}), bf16[1024,8,1664]{0,2,1:T(8,128)(2,1)}, u32[]{:S(2)}, u32[]{:S(2)}) async-start(bf16[1024,8,1664]{0,2,1:T(8,128)(2,1)} %bitcast.23), calls=%async_computation.1 | async-start | bytes 54525952 | tf_op jit(solution)/shard_map/all_to_all | solution.py:27
  1242.1 655.0 %all-gather.3.cloned.1.call-start = ((), (), s32[]{:S(2)}) async-start(), calls=%async_computation.4 | async-start | bytes 2359296 | tf_op jit(solution)/shard_map/all_gather | solution.py:32
  1243.1 667.4 %all-gather.5.cloned.1.call-start = ((), (), s32[]{:S(2)}) async-start(), calls=%async_computation.5 | async-start | bytes 2359296 | tf_op jit(solution)/shard_map/all_gather | solution.py:31
  1243.8 810.2 %reduce-scatter.2.cloned.1.call-start = ((), (), s32[]{:S(2)}) async-start(), calls=%async_computation.6 | async-start | bytes 4718592 | tf_op jit(solution)/shard_map/reduce_scatter | solution.py:39
  1910.4 14.4 copy-start
Sparse Core Ops, SparseCore 0:
  1245.1 472.9 all-gather.2
  1720.3 167.2 all-gather.4
  1967.2 86.7 reduce-scatter.1
where the time goes:
time: 2070 us
  waiting for transfers between devices  1190 us (57%)
  blocking collectives  605 us (29%)
  local copies, waits for them, and re-layouts  177 us (9%)
  matrix products  70 us (3%)
    all_to_all x1, blocking collectives, shards(): lax.all_to_all(gate_weight, 'gx', split_axis=1, concat_axis=0, tiled=True)  599 us
    all_to_all x1, waiting for transfers between devices, shards(): lax.all_to_all(down_weight, 'gx', split_axis=0, concat_axis=1, tiled=True)  551 us
    all_to_all x1, waiting for transfers between devices, shards(): lax.all_to_all(up_weight, 'gx', split_axis=1, concat_axis=0, tiled=True)  548 us
    reduce_scatter x1, waiting for transfers between devices, shards(): lax.psum_scatter(partial_grad, 'gx', scatter_dimension=1, tiled=True)  86.9 us
    unnamed x10, local copies, waits for them, and re-layouts  71.9 us
    dot_general x3, matrix products, transposed(): lax.dot_general(left, weight, (((1,), (1,)), ((), ())), preferred_element...  55.6 us
  transfers between devices with their start and end apart: 5, of which 3 were waited for; matrix products, arithmetic and copies ran while one was open for 8% of the time, Pallas kernels for 0%

commit v1 on v0

v1 whole, which is shorter than its diff:
```python
import jax
import jax.numpy as jnp
from jax import lax
from jax.sharding import PartitionSpec as P


def transposed(left, weight):
    return lax.dot_general(
        left, weight, (((1,), (1,)), ((), ())), preferred_element_type=jnp.float32
    )


def swiglu_grads(gate_proj, up_proj, hidden_grad):
    sigmoid_gate = jax.nn.sigmoid(gate_proj)
    gate_grad = hidden_grad * up_proj * sigmoid_gate * (1.0 + gate_proj * (1.0 - sigmoid_gate))
    up_grad = hidden_grad * gate_proj * sigmoid_gate
    return (gate_grad.astype(jnp.bfloat16), up_grad.astype(jnp.bfloat16))


def shards(activations, upstream, head_grad, target_mask, gate_weight, up_weight, down_weight):
    rows = activations.shape[0]
    weights_mask = target_mask.astype(jnp.float32)[:, None]
    cotangent = (
        upstream.astype(jnp.float32) + weights_mask * head_grad.astype(jnp.float32)
    ).astype(jnp.bfloat16)
    gate_part = jnp.dot(activations, gate_weight, preferred_element_type=jnp.float32)
    up_part = jnp.dot(activations, up_weight, preferred_element_type=jnp.float32)
    hidden_part = transposed(cotangent, down_weight)
    parts = jnp.concatenate([gate_part, up_part, hidden_part], axis=0)
    sums = lax.psum_scatter(parts, "gx", scatter_dimension=1, tiled=True)
    gate_grad, up_grad = swiglu_grads(sums[:rows], sums[rows : 2 * rows], sums[2 * rows :])
    grads = jnp.concatenate([gate_grad, up_grad], axis=0)
    whole = lax.all_gather(grads, "gx", axis=1, tiled=True)
    partial_grad = transposed(whole[:rows], gate_weight) + transposed(whole[rows:], up_weight)
    total_grad = lax.psum(partial_grad, "gy")
    return total_grad.astype(jnp.bfloat16)


def solution(mesh):
    in_specs = (
        P("grp", "gx"),
        P("grp", "gx"),
        P("grp", "gx"),
        P("grp"),
        P("gx", "gy"),
        P("gx", "gy"),
        P("gy", "gx"),
    )
    out_specs = P("grp", "gx")
    return jax.shard_map(shards, mesh=mesh, in_specs=in_specs, out_specs=out_specs, check_vma=False)
```

time: 2070 us -> 558 us (0.27)
  waiting for transfers between devices: 1190 us -> 443 us
  blocking collectives: 605 us -> 5.32 us
  local copies, waits for them, and re-layouts: 177 us -> 0.27 us
    all_to_all x2 -> x0, waiting for transfers between devices: 1100 us -> none  [the longest x1 551 us: shards(): lax.all_to_all(down_weight, 'gx', split_axis=0, concat_axis=1, tiled=True)]
    all_to_all x1 -> x0, blocking collectives: 599 us -> none  [shards(): lax.all_to_all(gate_weight, 'gx', split_axis=1, concat_axis=0, tiled=True)]
    reduce_scatter x1, waiting for transfers between devices: 86.9 us -> 338 us  [shards(): sums = lax.psum_scatter(parts, 'gx', scatter_dimension=1, tiled=True)]
    all_to_all x3 -> x0, local copies, waits for them, and re-layouts: 105 us -> none  [the longest x1 35.6 us: shards(): lax.all_to_all(gate_weight, 'gx', split_axis=1, concat_axis=0, tiled=True)]
    all_gather x2 -> x1, waiting for transfers between devices: 0.02 us -> 105 us  [shards(): whole = lax.all_gather(grads, 'gx', axis=1, tiled=True)]
    unnamed x10 -> x8, local copies, waits for them, and re-layouts: 71.9 us -> 0.27 us
  transfers between devices with their start and end apart: 5 -> 2, of which waited for: 3 -> 2; matrix products, arithmetic and copies ran while one was open for 8% -> 0% of each run, Pallas kernels for 0% -> 0%
where the time goes in v1:
time: 558 us
  waiting for transfers between devices  443 us (79%)
  matrix products  76.8 us (14%)
  other arithmetic  19.2 us (3%)
  between operations  13.4 us (2%)
    reduce_scatter x1, waiting for transfers between devices, shards(): sums = lax.psum_scatter(parts, 'gx', scatter_dimension=1, tiled=True)  338 us
    all_gather x1, waiting for transfers between devices, shards(): whole = lax.all_gather(grads, 'gx', axis=1, tiled=True)  105 us
    dot_general x3, matrix products, transposed(): lax.dot_general(left, weight, (((1,), (1,)), ((), ())), preferred_element...  46.3 us
    concatenate x1, other arithmetic, shards(): parts = jnp.concatenate([gate_part, up_part, hidden_part], axis=0)  15.5 us
    dot_general x1, matrix products, shards(): jnp.dot(activations, gate_weight, preferred_element_type=jnp.float32)  15.3 us
    dot_general x1, matrix products, shards(): jnp.dot(activations, up_weight, preferred_element_type=jnp.float32)  15.2 us
  transfers between devices with their start and end apart: 2, of which 2 were waited for; matrix products, arithmetic and copies ran while one was open for 0% of the time, Pallas kernels for 0%

profile of v1, /device:TPU:0, one launch (start us, length us, event | category | flops | bytes accessed | tf_op | source)
XLA Modules:
  0.0 558.1 jit_solution(820568350982471729)
XLA Ops:
  6.5 0.0 copy-start
  6.5 0.0 reduce-scatter.2.cloned.1.call-start
  6.5 0.7 convert_element_type.22
  7.2 0.3 copy-done
  7.5 15.2 %fusion.13 = f32[128,13312]{1,0:T(8,128)} fusion(bf16[128,1024]{1,0:T(8,128)(2,1)S(1)} %copy-done, bf16[1024,13312]{1,0:T(8,128)(2,1)} %param.12), kind=kOutput, calls=%fused_computation.17 | convolution fusion | flops 3489660928 | bytes 34340864 | tf_op jit(solution)/shard_map/dot_general | solution.py:27
  22.7 0.0 copy-start.2
  22.7 0.0 copy-start.3
  22.7 15.3 %fusion.12 = f32[128,13312]{1,0:T(8,128)} fusion(bf16[128,1024]{1,0:T(8,128)(2,1)S(1)} %copy-done, bf16[1024,13312]{1,0:T(8,128)(2,1)} %param.11), kind=kOutput, calls=%fused_computation.16 | convolution fusion | flops 3489660928 | bytes 34340864 | tf_op jit(solution)/shard_map/dot_general | solution.py:26
  38.0 0.0 copy-done.2
  38.0 0.0 copy-done.3
  38.0 15.8 %fusion.10 = f32[128,13312]{1,0:T(8,128)} fusion(bf16[13312,1024]{1,0:T(8,128)(2,1)} %param.13, bf16[128,1024]{1,0:T(8,128)(2,1)S(1)} %copy-done.2, bf16[128,1024]{1,0:T(8,128)(2,1)S(1)} %copy-done.3, f32[128]{0:T(128)S(1)} %convert_element_type.22), kind=kOutput, calls=%fused_computation.14 | convolution fusion | flops 3490316288 | bytes 34603520 | tf_op jit(solution)/shard_map/dot_general | solution.py:8
  53.8 15.5 %pad_maximum_fusion = f32[384,13312]{1,0:T(8,128)} fusion(f32[128,13312]{1,0:T(8,128)} %fusion.10, f32[128,13312]{1,0:T(8,128)} %fusion.13, f32[128,13312]{1,0:T(8,128)} %fusion.12), kind=kLoop, calls=%fused_computation | loop fusion | flops 10223616 | bytes 40894464 | tf_op jit(solution)/shard_map/concatenate | solution.py:29
  69.3 0.0 reduce-scatter.2.cloned.1.call-update
  69.4 0.2 all-gather.2.cloned.1.call-start
  69.6 338.0 %reduce-scatter.2.cloned.1.call-done = f32[384,1664]{1,0:T(8,128)} async-done(((f32[384,13312]{1,0:T(8,128)}), f32[384,1664]{1,0:T(8,128)}) %reduce-scatter.2.cloned.1.call-update) | async-done | bytes 2555920 | tf_op jit(solution)/shard_map/reduce_scatter | solution.py:30
  407.6 2.1 fusion.9
  409.6 1.0 pad_maximum_fusion.1
  410.6 0.0 all-gather.2.cloned.1.call-update
  410.6 104.9 %all-gather.2.cloned.1.call-done = bf16[256,13312]{1,0:T(8,128)(2,1)} async-done(((bf16[256,1664]{1,0:T(8,128)(2,1)}), bf16[256,13312]{1,0:T(8,128)(2,1)}) %all-gather.2.cloned.1.call-update) | async-done | bytes 6815760 | tf_op jit(solution)/shard_map/all_gather | solution.py:33
  515.5 0.0 copy-start.1
  515.5 15.2 %fusion = f32[128,1024]{1,0:T(8,128)S(1)} fusion(bf16[1024,13312]{1,0:T(8,128)(2,1)} %param.12, bf16[256,13312]{1,0:T(8,128)(2,1)} %all-gather.2.cloned.1.call-done), kind=kOutput, calls=%fused_computation.1 | convolution fusion | flops 3489660928 | bytes 31195136 | tf_op jit(solution)/shard_map/dot_general | solution.py:8
  530.7 15.2 %fusion.4 = f32[128,1024]{1,0:T(8,128)S(1)} fusion(f32[128,1024]{1,0:T(8,128)S(1)} %fusion, bf16[1024,13312]{1,0:T(8,128)(2,1)} %param.11, bf16[256,13312]{1,0:T(8,128)(2,1)} %all-gather.2.cloned.1.call-done), kind=kOutput, calls=%fused_computation.5 | convolution fusion | flops 3489792000 | bytes 31719424 | tf_op jit(solution)/shard_map/dot_general | solution.py:8
  546.0 5.3 all-reduce.1
  551.3 0.0 copy-done.1
Async XLA Ops:
  6.5 1.0 copy-start
  6.5 401.0 %reduce-scatter.2.cloned.1.call-start = ((), (), s32[]{:S(2)}) async-start(), calls=%async_computation.1 | async-start | bytes 23003136 | tf_op jit(solution)/shard_map/reduce_scatter | solution.py:30
  22.7 15.3 %copy-start.2 = (bf16[128,1024]{1,0:T(8,128)(2,1)S(1)}, bf16[128,1024]{1,0:T(8,128)(2,1)}, u32[]{:S(2)}) copy-start(bf16[128,1024]{1,0:T(8,128)(2,1)} %param.9) | copy-start | bytes 786436
  22.7 15.3 %copy-start.3 = (bf16[128,1024]{1,0:T(8,128)(2,1)S(1)}, bf16[128,1024]{1,0:T(8,128)(2,1)}, u32[]{:S(2)}) copy-start(bf16[128,1024]{1,0:T(8,128)(2,1)} %param.8) | copy-start | bytes 786436
  69.4 446.1 %all-gather.2.cloned.1.call-start = ((), (), s32[]{:S(2)}) async-start(), calls=%async_computation.2 | async-start | bytes 7667712 | tf_op jit(solution)/shard_map/all_gather | solution.py:33
  515.5 35.8 %copy-start.1 = (bf16[128,1024]{1,0:T(8,128)(2,1)S(1)}, bf16[128,1024]{1,0:T(8,128)(2,1)}, u32[]{:S(2)}) copy-start(bf16[128,1024]{1,0:T(8,128)(2,1)} %param.7) | copy-start | bytes 786436
Sparse Core Ops, SparseCore 0:
  69.5 338.0 reduce-scatter.1
  410.7 104.7 all-gather.1

commit v2 on v1

--- a/solution.py
+++ b/solution.py
@@ -1,7 +1,18 @@
+import functools
+
 import jax
 import jax.numpy as jnp
 from jax import lax
+from jax.experimental import pallas as pl
+from jax.experimental.pallas import tpu as pltpu
 from jax.sharding import PartitionSpec as P
+
+LANE = 128
+NX, NZ = 2, 4
+HALF = NZ * LANE
+CHUNK = NX * HALF
+LAG_B, LAG_C, LAG_D, LAG_E = 2, 3, 4, 5
+KEEP = 4
 
 
 def transposed(left, weight):
@@ -17,7 +28,7 @@
     return (gate_grad.astype(jnp.bfloat16), up_grad.astype(jnp.bfloat16))
 
 
-def shards(activations, upstream, head_grad, target_mask, gate_weight, up_weight, down_weight):
+def plain_shards(activations, upstream, head_grad, target_mask, gate_weight, up_weight, down_weight):
     rows = activations.shape[0]
     weights_mask = target_mask.astype(jnp.float32)[:, None]
     cotangent = (
@@ -36,7 +47,244 @@
     return total_grad.astype(jnp.bfloat16)
 
 
+def kernel(
+    steps, act_ref, ups_ref, head_ref, mask_ref, gate_hbm, up_hbm, down_hbm, out_ref,
+    cot, wg, wu, wd, eg, eu, psend, keep, xrecv, zsend, zrecv, grads, acc, other,
+    w_sem, e_sem, x_send, x_recv, z_send, z_recv, a_send, a_recv, d_send, d_recv, c_send, c_recv,
+):
+    rows = act_ref.shape[0]
+    grp, gx, gy = lax.axis_index("grp"), lax.axis_index("gx"), lax.axis_index("gy")
+    z, x = gx // NX, gx % NX
+    x_peer = (grp, z * NX + (1 - x), gy)
+    z_peer = [None] + [(grp, ((z + d) % NZ) * NX + x, gy) for d in range(1, NZ)]
+    core_peer = (grp, gx, 1 - gy)
+    mesh_id = dict(device_id_type=pl.DeviceIdType.MESH)
+
+    def cols(step):
+        return pl.ds(pl.multiple_of(step * CHUNK, CHUNK), CHUNK)
+
+    def weights_in(step):
+        slot = step % 2
+        return (
+            pltpu.make_async_copy(gate_hbm.at[:, cols(step)], wg.at[slot], w_sem.at[slot, 0]),
+            pltpu.make_async_copy(up_hbm.at[:, cols(step)], wu.at[slot], w_sem.at[slot, 1]),
+            pltpu.make_async_copy(down_hbm.at[cols(step), :], wd.at[slot], w_sem.at[slot, 2]),
+        )
+
+    def again_in(step):
+        slot = step % 2
+        return (
+            pltpu.make_async_copy(gate_hbm.at[:, cols(step)], eg.at[slot], e_sem.at[slot, 0]),
+            pltpu.make_async_copy(up_hbm.at[:, cols(step)], eu.at[slot], e_sem.at[slot, 1]),
+        )
+
+    def x_copy(k):
+        return pltpu.make_async_remote_copy(
+            psend.at[k], xrecv.at[k], x_send.at[k], x_recv.at[k], device_id=x_peer, **mesh_id
+        )
+
+    def z_copy(k, d):
+        return pltpu.make_async_remote_copy(
+            zsend.at[k, (z + d) % NZ], zrecv.at[k, d - 1], z_send.at[k, d - 1], z_recv.at[k, d - 1],
+            device_id=z_peer[d], **mesh_id
+        )
+
+    def piece(origin):
+        return pl.ds(pl.multiple_of(origin * LANE, LANE), LANE)
+
+    def a_copy(k, d, origin):
+        ref = grads.at[k, x, :, piece(origin)]
+        return pltpu.make_async_remote_copy(
+            ref, ref, a_send.at[k, d - 1], a_recv.at[k, d - 1], device_id=z_peer[d], **mesh_id
+        )
+
+    def d_copy(k, side):
+        ref = grads.at[k, side]
+        return pltpu.make_async_remote_copy(
+            ref, ref, d_send.at[k], d_recv.at[k], device_id=x_peer, **mesh_id
+        )
+
+    for copy in weights_in(0) + again_in(0):
+        copy.start()
+
+    barrier = pltpu.get_barrier_semaphore()
+    for peer in [x_peer, core_peer] + z_peer[1:]:
+        pl.semaphore_signal(barrier, inc=1, device_id=peer, **mesh_id)
+    pl.semaphore_wait(barrier, NZ + 1)
+
+    cot[...] = (
+        ups_ref[...].astype(jnp.float32) + mask_ref[...] * head_ref[...].astype(jnp.float32)
+    ).astype(jnp.bfloat16)
+    acc[...] = jnp.zeros_like(acc)
+
+    def stage_a(k):
+        for copy in weights_in(k):
+            copy.wait()
+
+        @pl.when(k + 1 < steps)
+        def _():
+            for copy in weights_in(k + 1):
+                copy.start()
+
+        slot = k % 2
+        for mine in (False, True):
+            side = x if mine else 1 - x
+            span = pl.ds(pl.multiple_of(side * HALF, HALF), HALF)
+            gate = jnp.dot(act_ref[...], wg[slot, :, span], preferred_element_type=jnp.float32)
+            up = jnp.dot(act_ref[...], wu[slot, :, span], preferred_element_type=jnp.float32)
+            hidden = transposed(cot[...], wd[slot, span, :])
+            for i, value in enumerate((gate, up, hidden)):
+                at = pl.ds(i * rows, rows)
+                if mine:
+                    keep[k % KEEP, at, :] = value
+                else:
+                    psend[k, at, :] = value.astype(jnp.bfloat16)
+            if not mine:
+                x_copy(k).start()
+
+    def stage_b(k):
+        x_copy(k).wait_recv()
+        for j in range(NZ):
+            at = pl.ds(j * LANE, LANE)
+            total = keep[k % KEEP, :, at] + xrecv[k, :, at].astype(jnp.float32)
+            keep[k % KEEP, :, at] = total
+            zsend[k, j] = total.astype(jnp.bfloat16)
+        for d in range(1, NZ):
+            z_copy(k, d).start()
+
+    def stage_c(k):
+        for d in range(1, NZ):
+            z_copy(k, d).wait_recv()
+        parts = []
+        for i in range(3):
+            at = pl.ds(i * rows, rows)
+            total = keep[k % KEEP, at, piece(z)]
+            for d in range(1, NZ):
+                total = total + zrecv[k, d - 1, at, :].astype(jnp.float32)
+            parts.append(total)
+        gate_grad, up_grad = swiglu_grads(*parts)
+        grads[k, x, pl.ds(0, rows), piece(z)] = gate_grad
+        grads[k, x, pl.ds(rows, rows), piece(z)] = up_grad
+        for d in range(1, NZ):
+            a_copy(k, d, z).start()
+
+    def stage_d(k):
+        for d in range(1, NZ):
+            a_copy(k, d, (z + NZ - d) % NZ).wait_recv()
+        d_copy(k, x).start()
+
+    def stage_e(k):
+        for copy in again_in(k):
+            copy.wait()
+
+        @pl.when(k + 1 < steps)
+        def _():
+            for copy in again_in(k + 1):
+                copy.start()
+
+        d_copy(k, 1 - x).wait_recv()
+        slot = k % 2
+        total = acc[...]
+        for side in range(NX):
+            span = pl.ds(side * HALF, HALF)
+            total += transposed(grads[k, side, pl.ds(0, rows), :], eg[slot, :, span])
+            total += transposed(grads[k, side, pl.ds(rows, rows), :], eu[slot, :, span])
+        acc[...] = total
+
+    def body(t, carry):
+        for lag, stage in (
+            (0, stage_a), (LAG_B, stage_b), (LAG_C, stage_c), (LAG_D, stage_d), (LAG_E, stage_e)
+        ):
+            @pl.when(jnp.logical_and(t >= lag, t < steps + lag))
+            def _():
+                stage(t - lag)
+        return carry
+
+    lax.fori_loop(0, steps + LAG_E, body, 0)
+
+    core = pltpu.make_async_remote_copy(acc, other, c_send, c_recv, device_id=core_peer, **mesh_id)
+    core.start()
+
+    def drain(k, carry):
+        x_copy(k).wait_send()
+        for d in range(1, NZ):
+            z_copy(k, d).wait_send()
+            a_copy(k, d, z).wait_send()
+        d_copy(k, x).wait_send()
+        return carry
+
+    lax.fori_loop(0, steps, drain, 0)
+    core.wait()
+    out_ref[...] = (acc[...] + other[...]).astype(out_ref.dtype)
+
+
+def kernel_shards(activations, upstream, head_grad, target_mask, gate_weight, up_weight, down_weight):
+    rows, features = activations.shape
+    hidden = gate_weight.shape[1]
+    steps = hidden // CHUNK
+    mask = target_mask.astype(jnp.float32)[:, None]
+    vmem = pl.BlockSpec(memory_space=pltpu.VMEM)
+    hbm = pl.BlockSpec(memory_space=pl.ANY)
+    dma = pltpu.SemaphoreType.DMA
+    bf16, f32 = jnp.bfloat16, jnp.float32
+    return pl.pallas_call(
+        functools.partial(kernel, steps),
+        out_shape=jax.ShapeDtypeStruct((rows, features), bf16),
+        in_specs=[vmem] * 4 + [hbm] * 3,
+        out_specs=vmem,
+        scratch_shapes=[
+            pltpu.VMEM((rows, features), bf16),
+            pltpu.VMEM((2, features, CHUNK), bf16),
+            pltpu.VMEM((2, features, CHUNK), bf16),
+            pltpu.VMEM((2, CHUNK, features), bf16),
+            pltpu.VMEM((2, features, CHUNK), bf16),
+            pltpu.VMEM((2, features, CHUNK), bf16),
+            pltpu.VMEM((steps, 3 * rows, HALF), bf16),
+            pltpu.VMEM((KEEP, 3 * rows, HALF), f32),
+            pltpu.VMEM((steps, 3 * rows, HALF), bf16),
+            pltpu.VMEM((steps, NZ, 3 * rows, LANE), bf16),
+            pltpu.VMEM((steps, NZ - 1, 3 * rows, LANE), bf16),
+            pltpu.VMEM((steps, NX, 2 * rows, HALF), bf16),
+            pltpu.VMEM((rows, features), f32),
+            pltpu.VMEM((rows, features), f32),
+            dma((2, 3)),
+            dma((2, 2)),
+            dma((steps,)),
+            dma((steps,)),
+            dma((steps, NZ - 1)),
+            dma((steps, NZ - 1)),
+            dma((steps, NZ - 1)),
+            dma((steps, NZ - 1)),
+            dma((steps,)),
+            dma((steps,)),
+            dma,
+            dma,
+        ],
+        compiler_params=pltpu.CompilerParams(
+            collective_id=0, has_side_effects=True, vmem_limit_bytes=60 * 2**20
+        ),
+        cost_estimate=pl.CostEstimate(
+            flops=10 * rows * features * hidden,
+            bytes_accessed=10 * features * hidden,
+            transcendentals=rows * hidden // 8,
+        ),
+    )(activations, upstream, head_grad, mask, gate_weight, up_weight, down_weight)
+
+
 def solution(mesh):
+    def shards(*arrays):
+        rows, features = arrays[0].shape
+        hidden = arrays[4].shape[1]
+        fits = (
+            mesh.shape["gx"] == NX * NZ
+            and mesh.shape["gy"] == 2
+            and hidden % CHUNK == 0
+            and hidden // CHUNK <= 13
+            and rows == 128
+            and features == 1024
+        )
+        return (kernel_shards if fits else plain_shards)(*arrays)
+
     in_specs = (
         P("grp", "gx"),
         P("grp", "gx"),

time: 558 us -> 218 us (0.39)
  waiting for transfers between devices: 443 us -> 0 us
  Pallas kernels: 0 us -> 214 us
  matrix products: 76.8 us -> 0 us
  other arithmetic: 19.2 us -> 0.66 us
  between operations: 13.4 us -> 0.01 us
    reduce_scatter x1 -> x0, waiting for transfers between devices: 338 us -> none  [shards(): sums = lax.psum_scatter(parts, 'gx', scatter_dimension=1, tiled=True)]
    pallas_call x0 -> x1, Pallas kernels: none -> 214 us  [kernel_shards(): pl.pallas_call(functools.partial(kernel, steps), out_shape=jax.ShapeDtype...]
    all_gather x1 -> x0, waiting for transfers between devices: 105 us -> none  [shards(): whole = lax.all_gather(grads, 'gx', axis=1, tiled=True)]
    dot_general x5 -> x0, matrix products: 76.8 us -> none  [the longest x3 46.3 us: transposed(): lax.dot_general(left, weight, (((1,), (1,)), ((), ())), preferred_element...]
    concatenate x2 -> x0, other arithmetic: 16.5 us -> none  [the longest x1 15.5 us: shards(): parts = jnp.concatenate([gate_part, up_part, hidden_part], axis=0)]
  transfers between devices with their start and end apart: 2 -> 0, of which waited for: 2 -> 0; matrix products, arithmetic and copies ran while one was open for 0% -> 0% of each run, Pallas kernels for 0% -> 0%
where the time goes in v2:
time: 218 us; the launch traced here: 217 us
  Pallas kernels  214 us (98%)
  local copies, waits for them, and re-layouts  2.41 us (1%)
    pallas_call x1, Pallas kernels, kernel_shards(): pl.pallas_call(functools.partial(kernel, steps), out_shape=jax.ShapeDtype...  214 us

profile of v2, /device:TPU:0, one launch (start us, length us, event | category | flops | bytes accessed | tf_op | source)
XLA Modules:
  0.0 217.1 jit_solution(2984517236572182672)
XLA Ops:
  0.0 0.7 convert_bitcast_fusion
  0.7 0.7 copy.8.mask_ref
  1.4 214.0 %shard_map.73 = bf16[128,1024]{1,0:T(8,128)(2,1)} custom-call(bf16[128,1024]{1,0:T(8,128)(2,1)} %act_ref.1, bf16[128,1024]{1,0:T(8,128)(2,1)} %ups_ref.1, bf16[128,1024]{1,0:T(8,128)(2,1)} %head_ref.1, f32[128,1]{1,0:T(8,128)} %copy.8.mask_ref, bf16[1024,13312]{1,0:T(8,128)(2,1)} %gate_hbm.1, bf16[1024,13312]{1,0:T(8,128)(2,1)} %up_hbm.1, ...), custom_call_target="tpu_custom_call" | custom-call | flops 17448304640 | bytes 136314880 | tf_op jit(solution)/shard_map/pallas_call | solution.py:230
  215.4 1.7 copy.10

commit v3 on v2

--- a/solution.py
+++ b/solution.py
@@ -11,7 +11,8 @@
 NX, NZ = 2, 4
 HALF = NZ * LANE
 CHUNK = NX * HALF
-LAG_B, LAG_C, LAG_D, LAG_E = 2, 3, 4, 5
+LAG_B, LAG_C, LAG_F, LAG_D, LAG_E = 1, 2, 3, 4, 5
+CYCLE = 5
 KEEP = 4
 
 
@@ -92,10 +93,49 @@
     def piece(origin):
         return pl.ds(pl.multiple_of(origin * LANE, LANE), LANE)
 
-    def a_copy(k, d, origin):
-        ref = grads.at[k, x, :, piece(origin)]
-        return pltpu.make_async_remote_copy(
-            ref, ref, a_send.at[k, d - 1], a_recv.at[k, d - 1], device_id=z_peer[d], **mesh_id
+    side_z, odd = z // 2, z % 2
+    inner = side_z + odd == 1
+    mate = (grp, (2 * side_z + 1 - odd) * NX + x, gy)
+    across = (grp, (2 - side_z) * NX + x, gy)
+
+    def early(k):
+        return (k % CYCLE) % 2 == 1
+
+    def both(k, run):
+        @pl.when(early(k))
+        def _():
+            run(True)
+
+        @pl.when(jnp.logical_not(early(k)))
+        def _():
+            run(False)
+
+    def gathered(k, first, span):
+        return grads.at[k, :, :, span] if first else grads.at[k, x, :, span]
+
+    def mate_copy(k, origin, first):
+        ref = gathered(k, first, piece(origin))
+        return pltpu.make_async_remote_copy(
+            ref, ref, a_send.at[k, 0], a_recv.at[k, 0], device_id=mate, **mesh_id
+        )
+
+    def across_copy(k, origin, first):
+        ref = gathered(k, first, piece(origin))
+        return pltpu.make_async_remote_copy(
+            ref, ref, a_send.at[k, 1], a_recv.at[k, 1 + origin % 2], device_id=across, **mesh_id
+        )
+
+    def pair_copy(k, side, first):
+        start = pl.multiple_of(side * 2 * LANE, 2 * LANE)
+        ref = gathered(k, first, pl.ds(start, 2 * LANE))
+        return pltpu.make_async_remote_copy(
+            ref, ref, a_send.at[k, 2], a_recv.at[k, 3], device_id=mate, **mesh_id
+        )
+
+    def own_copy(k, side):
+        ref = grads.at[k, side, :, piece(z)]
+        return pltpu.make_async_remote_copy(
+            ref, ref, d_send.at[k], d_recv.at[k], device_id=x_peer, **mesh_id
         )
 
     def d_copy(k, side):
@@ -165,13 +205,47 @@
         gate_grad, up_grad = swiglu_grads(*parts)
         grads[k, x, pl.ds(0, rows), piece(z)] = gate_grad
         grads[k, x, pl.ds(rows, rows), piece(z)] = up_grad
-        for d in range(1, NZ):
-            a_copy(k, d, z).start()
+
+        def send(first):
+            if first:
+                own_copy(k, x).start()
+            else:
+                mate_copy(k, z, first).start()
+                across_copy(k, z, first).start()
+
+        both(k, send)
+
+    def spread(k):
+        own_copy(k, 1 - x).wait_recv()
+        mate_copy(k, z, True).start()
+        across_copy(k, z, True).start()
+
+    def forward(k, first):
+        @pl.when(inner)
+        def _():
+            for i in range(2):
+                across_copy(k, 2 * (1 - side_z) + i, first).wait_recv()
+            pair_copy(k, 1 - side_z, first).start()
+
+    def arrived(k, first):
+        mate_copy(k, z, first).wait_recv()
+
+        @pl.when(jnp.logical_not(inner))
+        def _():
+            pair_copy(k, 1 - side_z, first).wait_recv()
+
+    def stage_f(k):
+        both(k, lambda first: spread(k) if first else forward(k, False))
 
     def stage_d(k):
-        for d in range(1, NZ):
-            a_copy(k, d, (z + NZ - d) % NZ).wait_recv()
-        d_copy(k, x).start()
+        def run(first):
+            if first:
+                forward(k, True)
+            else:
+                arrived(k, False)
+                d_copy(k, x).start()
+
+        both(k, run)
 
     def stage_e(k):
         for copy in again_in(k):
@@ -182,7 +256,7 @@
             for copy in again_in(k + 1):
                 copy.start()
 
-        d_copy(k, 1 - x).wait_recv()
+        both(k, lambda first: arrived(k, True) if first else d_copy(k, 1 - x).wait_recv())
         slot = k % 2
         total = acc[...]
         for side in range(NX):
@@ -193,7 +267,8 @@
 
     def body(t, carry):
         for lag, stage in (
-            (0, stage_a), (LAG_B, stage_b), (LAG_C, stage_c), (LAG_D, stage_d), (LAG_E, stage_e)
+            (0, stage_a), (LAG_B, stage_b), (LAG_C, stage_c),
+            (LAG_F, stage_f), (LAG_D, stage_d), (LAG_E, stage_e),
         ):
             @pl.when(jnp.logical_and(t >= lag, t < steps + lag))
             def _():
@@ -209,8 +284,18 @@
         x_copy(k).wait_send()
         for d in range(1, NZ):
             z_copy(k, d).wait_send()
-            a_copy(k, d, z).wait_send()
-        d_copy(k, x).wait_send()
+
+        def sent(first):
+            mate_copy(k, z, first).wait_send()
+            across_copy(k, z, first).wait_send()
+
+            @pl.when(inner)
+            def _():
+                pair_copy(k, 1 - side_z, first).wait_send()
+
+            (own_copy if first else d_copy)(k, x).wait_send()
+
+        both(k, sent)
         return carry
 
     lax.fori_loop(0, steps, drain, 0)
@@ -253,8 +338,8 @@
             dma((steps,)),
             dma((steps, NZ - 1)),
             dma((steps, NZ - 1)),
-            dma((steps, NZ - 1)),
-            dma((steps, NZ - 1)),
+            dma((steps, 3)),
+            dma((steps, 4)),
             dma((steps,)),
             dma((steps,)),
             dma,

time: 218 us -> 201 us (0.922)
  Pallas kernels: 214 us -> 197 us
    pallas_call x1, Pallas kernels: 214 us -> 197 us  [kernel_shards(): pl.pallas_call(functools.partial(kernel, steps), out_shape=jax.ShapeDtype...]
where the time goes in v3:
time: 201 us; the launch traced here: 200 us
  Pallas kernels  197 us (98%)
  local copies, waits for them, and re-layouts  2.41 us (1%)
    pallas_call x1, Pallas kernels, kernel_shards(): pl.pallas_call(functools.partial(kernel, steps), out_shape=jax.ShapeDtype...  197 us

profile of v3, /device:TPU:0, one launch (start us, length us, event | category | flops | bytes accessed | tf_op | source)
XLA Modules:
  0.0 199.9 jit_solution(976448621413986634)
XLA Ops:
  0.0 0.7 convert_bitcast_fusion
  0.7 0.7 copy.8.mask_ref
  1.4 196.8 %shard_map.73 = bf16[128,1024]{1,0:T(8,128)(2,1)} custom-call(bf16[128,1024]{1,0:T(8,128)(2,1)} %act_ref.1, bf16[128,1024]{1,0:T(8,128)(2,1)} %ups_ref.1, bf16[128,1024]{1,0:T(8,128)(2,1)} %head_ref.1, f32[128,1]{1,0:T(8,128)} %copy.8.mask_ref, bf16[1024,13312]{1,0:T(8,128)(2,1)} %gate_hbm.1, bf16[1024,13312]{1,0:T(8,128)(2,1)} %up_hbm.1, ...), custom_call_target="tpu_custom_call" | custom-call | flops 17448304640 | bytes 136314880 | tf_op jit(solution)/shard_map/pallas_call | solution.py:315
  198.2 1.7 copy.10

commit v4 on v3

--- a/solution.py
+++ b/solution.py
@@ -11,8 +11,8 @@
 NX, NZ = 2, 4
 HALF = NZ * LANE
 CHUNK = NX * HALF
-LAG_B, LAG_C, LAG_F, LAG_D, LAG_E = 1, 2, 3, 4, 5
-CYCLE = 5
+LAG_B, LAG_C, LAG_F, LAG_D, LAG_E = 2, 3, 4, 5, 6
+CYCLE = 3
 KEEP = 4
 
 
@@ -99,7 +99,7 @@
     across = (grp, (2 - side_z) * NX + x, gy)
 
     def early(k):
-        return (k % CYCLE) % 2 == 1
+        return k % CYCLE == 0
 
     def both(k, run):
         @pl.when(early(k))

time: 201 us -> 199 us (0.990)
  no operation moved by 1% of the time
where the time goes in v4:
time: 199 us
  Pallas kernels  196 us (98%)
  local copies, waits for them, and re-layouts  2.41 us (1%)
    pallas_call x1, Pallas kernels, kernel_shards(): pl.pallas_call(functools.partial(kernel, steps), out_shape=jax.ShapeDtype...  196 us

profile of v4, /device:TPU:0, one launch (start us, length us, event | category | flops | bytes accessed | tf_op | source)
XLA Modules:
  0.0 199.0 jit_solution(14852850958488327167)
XLA Ops:
  0.0 0.7 convert_bitcast_fusion
  0.7 0.7 copy.8.mask_ref
  1.4 195.9 %shard_map.73 = bf16[128,1024]{1,0:T(8,128)(2,1)} custom-call(bf16[128,1024]{1,0:T(8,128)(2,1)} %act_ref.1, bf16[128,1024]{1,0:T(8,128)(2,1)} %ups_ref.1, bf16[128,1024]{1,0:T(8,128)(2,1)} %head_ref.1, f32[128,1]{1,0:T(8,128)} %copy.8.mask_ref, bf16[1024,13312]{1,0:T(8,128)(2,1)} %gate_hbm.1, bf16[1024,13312]{1,0:T(8,128)(2,1)} %up_hbm.1, ...), custom_call_target="tpu_custom_call" | custom-call | flops 17448304640 | bytes 136314880 | tf_op jit(solution)/shard_map/pallas_call | solution.py:315
  197.4 1.7 copy.10
